TPU v7x, 128 devices: a whole 4x4x4 slice. The times are simulated.
128 devices in a mesh: dom: 16 (over x, z_hi, core), space: 8 (over y, z_lo).
Axes of the slice: x: 4, y: 4, z: 4 (z_hi: 2, z_lo: 2; z = z_hi * 2 + z_lo), core: 2. Of those that a mesh axis runs over, the one named last changes fastest.
Arguments:
- particles: float32 [32, 3, 512, 1024], P('dom', None, 'space'), may hold values from -6 to 6
- copies: int32 [32], replicated, may hold values from 0 to 31
- depth_class: int32 [512, 1024], P('space'), may hold values from 0 to 7
- depth_table: float32 [8], replicated, may hold values from 0.5 to 2
- observed: float32 [512, 1024], P('space'), may hold values from -6 to 6
- nudge_gain: float32 [512, 1024], P('space'), may hold values from 0.02 to 0.3
Outputs:
- advanced: float32 [32, 3, 512, 1024], P('dom', None, 'space')
All inputs are finite; a program needn't handle non-finite values.
Results may differ from a plain program's by a relative error of at most 0.00002.
Values sent between devices are 32-bit elements; how exact they have to be, the bound alone decides.
A program may use at most 128 MiB of HBM per device.

v0:
```python
import jax
import jax.numpy as jnp
from jax import lax
from jax.sharding import PartitionSpec as P

STEPS = 4


time_step = 0.3
coriolis = 0.3


def extended(block, sides, width):
    for axis, dim in sides:
        count = lax.axis_size(axis)
        forward = [(i, i + 1) for i in range(count - 1)]
        backward = [(target, source) for source, target in forward]
        low = lax.ppermute(
            lax.slice_in_dim(block, block.shape[dim] - width, None, axis=dim), axis, forward
        )
        high = lax.ppermute(lax.slice_in_dim(block, 0, width, axis=dim), axis, backward)
        block = jnp.concatenate([low, block, high], axis=dim)
    return block


def depth_of(depth_class, depth_table):
    depth = jnp.zeros(depth_class.shape, jnp.float32)
    for klass in range(depth_table.shape[0]):
        depth = jnp.where(depth_class == klass, depth_table[klass], depth)
    return depth


def col_diff(field):
    ahead = jnp.roll(field, -1, axis=-1)
    behind = jnp.roll(field, 1, axis=-1)
    ahead_two = jnp.roll(field, -2, axis=-1)
    behind_two = jnp.roll(field, 2, axis=-1)
    return (8.0 * (ahead - behind) - (ahead_two - behind_two)) / 12.0


def row_diff(padded):
    return (
        8.0 * (padded[..., 3:-1, :] - padded[..., 1:-3, :])
        - (padded[..., 4:, :] - padded[..., :-4, :])
    ) / 12.0


def shards(particles, copies, depth_class, depth_table, observed, nudge_gain):
    per_dev = particles.shape[0]
    dom_index = lax.axis_index("dom")
    my_sources = lax.dynamic_slice_in_dim(copies, dom_index * per_dev, per_dev)
    piece = lax.all_gather(particles, "dom", axis=0, tiled=True)
    count = piece.shape[0]
    inside = (my_sources >= 0) & (my_sources < count)
    taken = jnp.take(piece, jnp.clip(my_sources, 0, count - 1), axis=0)
    state = jnp.where(inside[:, None, None, None], taken, jnp.zeros(particles.shape, jnp.float32))
    depth = depth_of(depth_class, depth_table)
    height, east_vel, north_vel = (state[:, 0], state[:, 1], state[:, 2])
    for _ in range(STEPS):
        fluxes = jnp.stack([depth * east_vel, depth * north_vel], axis=1)
        flux_ext = extended(fluxes, (("space", 2),), 2)
        spread_div = col_diff(fluxes[:, 0]) + row_diff(flux_ext[:, 1])
        height = height - time_step * spread_div
        height = height + nudge_gain * (observed - height)
        height_ext = extended(height, (("space", 1),), 2)
        new_east = east_vel + time_step * (-col_diff(height) + coriolis * north_vel)
        north_vel = north_vel + time_step * (-row_diff(height_ext) - coriolis * east_vel)
        east_vel = new_east
    result = jnp.stack([height, east_vel, north_vel], axis=1)
    return result


def solution(mesh):
    placed = (
        P("dom", None, "space", None),
        P(),
        P("space", None),
        P(),
        P("space", None),
        P("space", None),
    )
    return jax.shard_map(
        shards, mesh=mesh, in_specs=placed, out_specs=P("dom", None, "space", None), check_vma=False
    )
```

profile of v0, /device:TPU:16, one launch (start us, length us, event | category | flops | bytes accessed | tf_op | source)
XLA Modules:
  0.0 268.2 jit_solution(11669681949942031623)
XLA Ops:
  6.5 0.7 all-gather.2.cloned.1.call-update
  7.4 0.7 fusion.153
  8.1 5.2 %select_select_fusion.1 = f32[64,1024]{1,0:T(8,128)S(1)} fusion(s32[64,1024]{1,0:T(8,128)S(1)} %copy-done.2, f32[]{:T(128)} %bitcast.8, f32[]{:T(128)} %bitcast.7, f32[]{:T(128)} %bitcast.6, f32[]{:T(128)} %bitcast.5, f32[]{:T(128)} %bitcast.4, f32[]{:T(128)} %bitcast.3, f32[]{:T(128)} %bitcast.2, f32[]{:T(128)} %bitcast.1), kind=kLoop, calls=%fused_computation.196 | loop fusion | flops 1048576 | bytes 524320 | tf_op jit(solution)/shard_map/jit(_where)/select_n | solution.py:29
  13.2 147.7 %all-gather.2.cloned.1.call-done = f32[32,3,64,1024]{3,2,1,0:T(8,128)} async-done(((f32[2,3,64,1024]{3,2,1,0:T(8,128)}), f32[32,3,64,1024]{3,2,1,0:T(8,128)}) %all-gather.2.cloned.1.call-update) | async-done | bytes 25165840 | tf_op jit(solution)/shard_map/all_gather | solution.py:52
  161.0 8.8 %gather_fusion = f32[2,3,64,1024]{3,2,1,0:T(8,128)S(1)} fusion(f32[32,3,64,1024]{3,2,1,0:T(8,128)} %all-gather.2.cloned.1.call-done, s32[1024]{0:T(1024)S(1)} %pad_clamp_fusion), kind=kCustom, calls=%fused_computation | custom fusion | bytes 3145736 | tf_op jit(solution)/shard_map/jit(_take)/gather | solution.py:55
  169.8 0.3 select_select_fusion
  170.8 2.7 %collective-permute-start = (f32[2,2,2,1024]{3,2,0,1:T(2,128)S(1)}, f32[2,2,2,1024]{3,2,0,1:T(2,128)S(1)}, u32[]{:S(2)}, u32[]{:S(2)}) collective-permute-start(f32[2,2,2,1024]{3,2,0,1:T(2,128)S(1)} %get-tuple-element.33), channel_id=1, source_target_pairs={{0,1},{1,2},{2,3},{3,4},{4,5},{5,6},{6,7},{8,9},{9,10},{10,11},{11... | collective-permute-start | bytes 98312 | tf_op jit(solution)/shard_map/ppermute | solution.py:18
  173.5 4.2 %collective-permute-start.1 = (f32[2,2,2,1024]{3,2,0,1:T(2,128)S(1)}, f32[2,2,2,1024]{3,2,0,1:T(2,128)S(1)}, u32[]{:S(2)}, u32[]{:S(2)}) collective-permute-start(f32[2,2,2,1024]{3,2,0,1:T(2,128)S(1)} %get-tuple-element.34), channel_id=1, source_target_pairs={{1,0},{2,1},{3,2},{4,3},{5,4},{6,5},{7,6},{9,8},{10,9},{11,10},{12... | collective-permute-start | bytes 98312 | tf_op jit(solution)/shard_map/ppermute | solution.py:21
  177.8 1.5 collective-permute-done.1
  179.5 0.5 multiply_add_fusion.3
  180.1 0.2 slice_bitcast_fusion.5
  180.4 0.2 slice_bitcast_fusion.7
  180.6 0.5 broadcast_multiply_fusion.2
  181.5 5.1 %collective-permute-start.2 = (f32[2,2,1024]{2,1,0:T(2,128)S(1)}, f32[2,2,1024]{2,1,0:T(2,128)S(1)}, u32[]{:S(2)}, u32[]{:S(2)}) collective-permute-start(f32[2,2,1024]{2,1,0:T(2,128)S(1)} %get-tuple-element.105), channel_id=1, source_target_pairs={{1,0},{2,1},{3,2},{4,3},{5,4},{6,5},{7,6},{9,8},{10,9},{11,10},{12... | collective-permute-start | bytes 49160 | tf_op jit(solution)/shard_map/ppermute | solution.py:21
  186.6 1.9 collective-permute-start.3
  188.5 0.5 fusion.88
  189.1 4.0 %collective-permute-done.3 = f32[2,2,1024]{2,1,0:T(2,128)S(1)} collective-permute-done((f32[2,2,1024]{2,1,0:T(2,128)S(1)}, f32[2,2,1024]{2,1,0:T(2,128)S(1)}, u32[]{:S(2)}, u32[]{:S(2)}) %collective-permute-start.3) | collective-permute-done | bytes 16416 | tf_op jit(solution)/shard_map/ppermute | solution.py:18
  193.1 0.3 multiply_bitcast_fusion.2
  193.5 1.9 collective-permute-start.4
  195.4 4.8 %collective-permute-start.5 = (f32[2,2,2,1024]{3,2,1,0:T(2,128)S(1)}, f32[2,2,2,1024]{3,2,1,0:T(2,128)S(1)}, u32[]{:S(2)}, u32[]{:S(2)}) collective-permute-start(f32[2,2,2,1024]{3,2,1,0:T(2,128)S(1)} %get-tuple-element.32), channel_id=1, source_target_pairs={{1,0},{2,1},{3,2},{4,3},{5,4},{6,5},{7,6},{9,8},{10,9},{11,10},{12... | collective-permute-start | bytes 98312 | tf_op jit(solution)/shard_map/ppermute | solution.py:21
  200.3 1.5 collective-permute-done.5
  201.9 0.5 multiply_add_fusion.2
  203.0 5.1 %collective-permute-start.6 = (f32[2,2,1024]{2,1,0:T(2,128)S(1)}, f32[2,2,1024]{2,1,0:T(2,128)S(1)}, u32[]{:S(2)}, u32[]{:S(2)}) collective-permute-start(f32[2,2,1024]{2,1,0:T(2,128)S(1)} %get-tuple-element.79), channel_id=1, source_target_pairs={{1,0},{2,1},{3,2},{4,3},{5,4},{6,5},{7,6},{9,8},{10,9},{11,10},{12... | collective-permute-start | bytes 49160 | tf_op jit(solution)/shard_map/ppermute | solution.py:21
  208.1 1.9 collective-permute-start.7
  210.1 4.5 %collective-permute-done.7 = f32[2,2,1024]{2,1,0:T(2,128)S(1)} collective-permute-done((f32[2,2,1024]{2,1,0:T(2,128)S(1)}, f32[2,2,1024]{2,1,0:T(2,128)S(1)}, u32[]{:S(2)}, u32[]{:S(2)}) %collective-permute-start.7) | collective-permute-done | bytes 16416 | tf_op jit(solution)/shard_map/ppermute | solution.py:18
  214.6 0.6 broadcast_multiply_fusion.1
  215.3 0.2 fusion.137
  215.5 0.2 fusion.135
  215.8 1.9 collective-permute-start.8
  217.7 4.8 %collective-permute-start.9 = (f32[2,2,2,1024]{3,2,0,1:T(2,128)S(1)}, f32[2,2,2,1024]{3,2,0,1:T(2,128)S(1)}, u32[]{:S(2)}, u32[]{:S(2)}) collective-permute-start(f32[2,2,2,1024]{3,2,0,1:T(2,128)S(1)} %get-tuple-element.30), channel_id=1, source_target_pairs={{1,0},{2,1},{3,2},{4,3},{5,4},{6,5},{7,6},{9,8},{10,9},{11,10},{12... | collective-permute-start | bytes 98312 | tf_op jit(solution)/shard_map/ppermute | solution.py:21
  222.6 1.6 collective-permute-done.9
  224.3 0.5 multiply_add_fusion.1
  225.3 5.1 %collective-permute-start.10 = (f32[2,2,1024]{2,1,0:T(2,128)S(1)}, f32[2,2,1024]{2,1,0:T(2,128)S(1)}, u32[]{:S(2)}, u32[]{:S(2)}) collective-permute-start(f32[2,2,1024]{2,1,0:T(2,128)S(1)} %get-tuple-element.61), channel_id=1, source_target_pairs={{1,0},{2,1},{3,2},{4,3},{5,4},{6,5},{7,6},{9,8},{10,9},{11,10},{12... | collective-permute-start | bytes 49160 | tf_op jit(solution)/shard_map/ppermute | solution.py:21
  230.4 1.9 collective-permute-start.11
  232.4 4.6 %collective-permute-done.11 = f32[2,2,1024]{2,1,0:T(2,128)S(1)} collective-permute-done((f32[2,2,1024]{2,1,0:T(2,128)S(1)}, f32[2,2,1024]{2,1,0:T(2,128)S(1)}, u32[]{:S(2)}, u32[]{:S(2)}) %collective-permute-start.11) | collective-permute-done | bytes 16416 | tf_op jit(solution)/shard_map/ppermute | solution.py:18
  237.1 0.6 broadcast_multiply_fusion
  237.8 0.2 fusion.128
  238.0 0.2 fusion.126
  238.2 1.9 collective-permute-start.12
  240.2 4.8 %collective-permute-start.13 = (f32[2,2,2,1024]{3,2,0,1:T(2,128)S(1)}, f32[2,2,2,1024]{3,2,0,1:T(2,128)S(1)}, u32[]{:S(2)}, u32[]{:S(2)}) collective-permute-start(f32[2,2,2,1024]{3,2,0,1:T(2,128)S(1)} %get-tuple-element.28), channel_id=1, source_target_pairs={{1,0},{2,1},{3,2},{4,3},{5,4},{6,5},{7,6},{9,8},{10,9},{11,10},{12... | collective-permute-start | bytes 98312 | tf_op jit(solution)/shard_map/ppermute | solution.py:21
  245.1 1.5 collective-permute-done.13
  246.7 0.5 multiply_add_fusion
  247.5 0.2 fusion.122
  247.7 5.1 %collective-permute-start.14 = (f32[2,2,1024]{2,1,0:T(2,128)S(1)}, f32[2,2,1024]{2,1,0:T(2,128)S(1)}, u32[]{:S(2)}, u32[]{:S(2)}) collective-permute-start(f32[2,2,1024]{2,1,0:T(2,128)S(1)} %get-tuple-element.43), channel_id=1, source_target_pairs={{1,0},{2,1},{3,2},{4,3},{5,4},{6,5},{7,6},{9,8},{10,9},{11,10},{12... | collective-permute-start | bytes 49160 | tf_op jit(solution)/shard_map/ppermute | solution.py:21
  252.8 1.9 collective-permute-start.15
  254.8 4.5 %collective-permute-done.15 = f32[2,2,1024]{2,1,0:T(2,128)S(1)} collective-permute-done((f32[2,2,1024]{2,1,0:T(2,128)S(1)}, f32[2,2,1024]{2,1,0:T(2,128)S(1)}, u32[]{:S(2)}, u32[]{:S(2)}) %collective-permute-start.15) | collective-permute-done | bytes 16416 | tf_op jit(solution)/shard_map/ppermute | solution.py:18
  259.3 0.6 fusion.114
  260.1 1.3 copy.30
  (61 shorter events, 4.1 us)
Async XLA Ops:
  6.5 0.7 copy-start.4
  6.5 0.8 copy-start.3
  6.5 1.5 copy-start.2
  6.5 154.4 %all-gather.2.cloned.1.call-start = ((), (), s32[]{:S(2)}) async-start(), calls=%async_computation | async-start | bytes 26738688 | tf_op jit(solution)/shard_map/all_gather | solution.py:52
  170.8 8.7 %copy-start = (f32[64,1024]{1,0:T(8,128)S(1)}, f32[64,1024]{1,0:T(8,128)}, u32[]{:S(2)}) copy-start(f32[64,1024]{1,0:T(8,128)} %param.10) | copy-start | bytes 786436
  170.8 8.7 %copy-start.1 = (f32[64,1024]{1,0:T(8,128)S(1)}, f32[64,1024]{1,0:T(8,128)}, u32[]{:S(2)}) copy-start(f32[64,1024]{1,0:T(8,128)} %param.11) | copy-start | bytes 786436
  170.8 7.0 %collective-permute-start = (f32[2,2,2,1024]{3,2,0,1:T(2,128)S(1)}, f32[2,2,2,1024]{3,2,0,1:T(2,128)S(1)}, u32[]{:S(2)}, u32[]{:S(2)}) collective-permute-start(f32[2,2,2,1024]{3,2,0,1:T(2,128)S(1)} %get-tuple-element.33), channel_id=1, source_target_pairs={{0,1},{1,2},{2,3},{3,4},{4,5},{5,6},{6,7},{8,9},{9,10},{10,11},{11... | collective-permute-start | bytes 98312 | tf_op jit(solution)/shard_map/ppermute | solution.py:18
  173.5 5.8 %collective-permute-start.1 = (f32[2,2,2,1024]{3,2,0,1:T(2,128)S(1)}, f32[2,2,2,1024]{3,2,0,1:T(2,128)S(1)}, u32[]{:S(2)}, u32[]{:S(2)}) collective-permute-start(f32[2,2,2,1024]{3,2,0,1:T(2,128)S(1)} %get-tuple-element.34), channel_id=1, source_target_pairs={{1,0},{2,1},{3,2},{4,3},{5,4},{6,5},{7,6},{9,8},{10,9},{11,10},{12... | collective-permute-start | bytes 98312 | tf_op jit(solution)/shard_map/ppermute | solution.py:21
  181.5 7.6 %collective-permute-start.2 = (f32[2,2,1024]{2,1,0:T(2,128)S(1)}, f32[2,2,1024]{2,1,0:T(2,128)S(1)}, u32[]{:S(2)}, u32[]{:S(2)}) collective-permute-start(f32[2,2,1024]{2,1,0:T(2,128)S(1)} %get-tuple-element.105), channel_id=1, source_target_pairs={{1,0},{2,1},{3,2},{4,3},{5,4},{6,5},{7,6},{9,8},{10,9},{11,10},{12... | collective-permute-start | bytes 49160 | tf_op jit(solution)/shard_map/ppermute | solution.py:21
  186.6 6.5 %collective-permute-start.3 = (f32[2,2,1024]{2,1,0:T(2,128)S(1)}, f32[2,2,1024]{2,1,0:T(2,128)S(1)}, u32[]{:S(2)}, u32[]{:S(2)}) collective-permute-start(f32[2,2,1024]{2,1,0:T(2,128)S(1)} %get-tuple-element.106), channel_id=1, source_target_pairs={{0,1},{1,2},{2,3},{3,4},{4,5},{5,6},{6,7},{8,9},{9,10},{10,11},{11... | collective-permute-start | bytes 49160 | tf_op jit(solution)/shard_map/ppermute | solution.py:18
  193.5 6.8 %collective-permute-start.4 = (f32[2,2,2,1024]{3,2,1,0:T(2,128)S(1)}, f32[2,2,2,1024]{3,2,1,0:T(2,128)S(1)}, u32[]{:S(2)}, u32[]{:S(2)}) collective-permute-start(f32[2,2,2,1024]{3,2,1,0:T(2,128)S(1)} %get-tuple-element.31), channel_id=1, source_target_pairs={{0,1},{1,2},{2,3},{3,4},{4,5},{5,6},{6,7},{8,9},{9,10},{10,11},{11... | collective-permute-start | bytes 98312 | tf_op jit(solution)/shard_map/ppermute | solution.py:18
  195.4 6.4 %collective-permute-start.5 = (f32[2,2,2,1024]{3,2,1,0:T(2,128)S(1)}, f32[2,2,2,1024]{3,2,1,0:T(2,128)S(1)}, u32[]{:S(2)}, u32[]{:S(2)}) collective-permute-start(f32[2,2,2,1024]{3,2,1,0:T(2,128)S(1)} %get-tuple-element.32), channel_id=1, source_target_pairs={{1,0},{2,1},{3,2},{4,3},{5,4},{6,5},{7,6},{9,8},{10,9},{11,10},{12... | collective-permute-start | bytes 98312 | tf_op jit(solution)/shard_map/ppermute | solution.py:21
  203.0 7.1 %collective-permute-start.6 = (f32[2,2,1024]{2,1,0:T(2,128)S(1)}, f32[2,2,1024]{2,1,0:T(2,128)S(1)}, u32[]{:S(2)}, u32[]{:S(2)}) collective-permute-start(f32[2,2,1024]{2,1,0:T(2,128)S(1)} %get-tuple-element.79), channel_id=1, source_target_pairs={{1,0},{2,1},{3,2},{4,3},{5,4},{6,5},{7,6},{9,8},{10,9},{11,10},{12... | collective-permute-start | bytes 49160 | tf_op jit(solution)/shard_map/ppermute | solution.py:21
  208.1 6.5 %collective-permute-start.7 = (f32[2,2,1024]{2,1,0:T(2,128)S(1)}, f32[2,2,1024]{2,1,0:T(2,128)S(1)}, u32[]{:S(2)}, u32[]{:S(2)}) collective-permute-start(f32[2,2,1024]{2,1,0:T(2,128)S(1)} %get-tuple-element.80), channel_id=1, source_target_pairs={{0,1},{1,2},{2,3},{3,4},{4,5},{5,6},{6,7},{8,9},{9,10},{10,11},{11... | collective-permute-start | bytes 49160 | tf_op jit(solution)/shard_map/ppermute | solution.py:18
  215.8 6.8 %collective-permute-start.8 = (f32[2,2,2,1024]{3,2,0,1:T(2,128)S(1)}, f32[2,2,2,1024]{3,2,0,1:T(2,128)S(1)}, u32[]{:S(2)}, u32[]{:S(2)}) collective-permute-start(f32[2,2,2,1024]{3,2,0,1:T(2,128)S(1)} %get-tuple-element.29), channel_id=1, source_target_pairs={{0,1},{1,2},{2,3},{3,4},{4,5},{5,6},{6,7},{8,9},{9,10},{10,11},{11... | collective-permute-start | bytes 98312 | tf_op jit(solution)/shard_map/ppermute | solution.py:18
  217.7 6.6 %collective-permute-start.9 = (f32[2,2,2,1024]{3,2,0,1:T(2,128)S(1)}, f32[2,2,2,1024]{3,2,0,1:T(2,128)S(1)}, u32[]{:S(2)}, u32[]{:S(2)}) collective-permute-start(f32[2,2,2,1024]{3,2,0,1:T(2,128)S(1)} %get-tuple-element.30), channel_id=1, source_target_pairs={{1,0},{2,1},{3,2},{4,3},{5,4},{6,5},{7,6},{9,8},{10,9},{11,10},{12... | collective-permute-start | bytes 98312 | tf_op jit(solution)/shard_map/ppermute | solution.py:21
  225.3 7.1 %collective-permute-start.10 = (f32[2,2,1024]{2,1,0:T(2,128)S(1)}, f32[2,2,1024]{2,1,0:T(2,128)S(1)}, u32[]{:S(2)}, u32[]{:S(2)}) collective-permute-start(f32[2,2,1024]{2,1,0:T(2,128)S(1)} %get-tuple-element.61), channel_id=1, source_target_pairs={{1,0},{2,1},{3,2},{4,3},{5,4},{6,5},{7,6},{9,8},{10,9},{11,10},{12... | collective-permute-start | bytes 49160 | tf_op jit(solution)/shard_map/ppermute | solution.py:21
  230.4 6.6 %collective-permute-start.11 = (f32[2,2,1024]{2,1,0:T(2,128)S(1)}, f32[2,2,1024]{2,1,0:T(2,128)S(1)}, u32[]{:S(2)}, u32[]{:S(2)}) collective-permute-start(f32[2,2,1024]{2,1,0:T(2,128)S(1)} %get-tuple-element.62), channel_id=1, source_target_pairs={{0,1},{1,2},{2,3},{3,4},{4,5},{5,6},{6,7},{8,9},{9,10},{10,11},{11... | collective-permute-start | bytes 49160 | tf_op jit(solution)/shard_map/ppermute | solution.py:18
  238.2 6.8 %collective-permute-start.12 = (f32[2,2,2,1024]{3,2,0,1:T(2,128)S(1)}, f32[2,2,2,1024]{3,2,0,1:T(2,128)S(1)}, u32[]{:S(2)}, u32[]{:S(2)}) collective-permute-start(f32[2,2,2,1024]{3,2,0,1:T(2,128)S(1)} %get-tuple-element.27), channel_id=1, source_target_pairs={{0,1},{1,2},{2,3},{3,4},{4,5},{5,6},{6,7},{8,9},{9,10},{10,11},{11... | collective-permute-start | bytes 98312 | tf_op jit(solution)/shard_map/ppermute | solution.py:18
  240.2 6.4 %collective-permute-start.13 = (f32[2,2,2,1024]{3,2,0,1:T(2,128)S(1)}, f32[2,2,2,1024]{3,2,0,1:T(2,128)S(1)}, u32[]{:S(2)}, u32[]{:S(2)}) collective-permute-start(f32[2,2,2,1024]{3,2,0,1:T(2,128)S(1)} %get-tuple-element.28), channel_id=1, source_target_pairs={{1,0},{2,1},{3,2},{4,3},{5,4},{6,5},{7,6},{9,8},{10,9},{11,10},{12... | collective-permute-start | bytes 98312 | tf_op jit(solution)/shard_map/ppermute | solution.py:21
  247.7 7.1 %collective-permute-start.14 = (f32[2,2,1024]{2,1,0:T(2,128)S(1)}, f32[2,2,1024]{2,1,0:T(2,128)S(1)}, u32[]{:S(2)}, u32[]{:S(2)}) collective-permute-start(f32[2,2,1024]{2,1,0:T(2,128)S(1)} %get-tuple-element.43), channel_id=1, source_target_pairs={{1,0},{2,1},{3,2},{4,3},{5,4},{6,5},{7,6},{9,8},{10,9},{11,10},{12... | collective-permute-start | bytes 49160 | tf_op jit(solution)/shard_map/ppermute | solution.py:21
  252.8 6.5 %collective-permute-start.15 = (f32[2,2,1024]{2,1,0:T(2,128)S(1)}, f32[2,2,1024]{2,1,0:T(2,128)S(1)}, u32[]{:S(2)}, u32[]{:S(2)}) collective-permute-start(f32[2,2,1024]{2,1,0:T(2,128)S(1)} %get-tuple-element.44), channel_id=1, source_target_pairs={{0,1},{1,2},{2,3},{3,4},{4,5},{5,6},{6,7},{8,9},{9,10},{10,11},{11... | collective-permute-start | bytes 49160 | tf_op jit(solution)/shard_map/ppermute | solution.py:18
Sparse Core Ops, SparseCore 0:
  9.8 151.1 all-gather.1
where the time goes:
time: 269 us; the launch traced here: 268 us
  waiting for transfers between devices  172 us (64%)
  starting transfers between devices  55.2 us (21%)
  local copies, waits for them, and re-layouts  15.5 us (6%)
  between operations  13.8 us (5%)
  other arithmetic  11.4 us (4%)
    all_gather x1, waiting for transfers between devices, shards(): piece = lax.all_gather(particles, 'dom', axis=0, tiled=True)  148 us
    ppermute x8, starting transfers between devices, extended(): lax.ppermute(lax.slice_in_dim(block, 0, width, axis=dim), axis, backward)  39 us
    ppermute x8, waiting for transfers between devices, extended(): lax.ppermute(lax.slice_in_dim(block, block.shape[dim] - width, None, axis...  17.7 us
    ppermute x8, starting transfers between devices, extended(): lax.ppermute(lax.slice_in_dim(block, block.shape[dim] - width, None, axis...  16.1 us
    gather x1, local copies, waits for them, and re-layouts, shards(): taken = jnp.take(piece, jnp.clip(my_sources, 0, count - 1), axis=0)  8.8 us
    ppermute x8, waiting for transfers between devices, extended(): lax.ppermute(lax.slice_in_dim(block, 0, width, axis=dim), axis, backward)  6.19 us
  transfers between devices with their start and end apart: 17, of which 9 were waited for; matrix products, arithmetic and copies ran while one was open for 3% of the time, Pallas kernels for 0%

commit v1 on v0

v1 whole, which is shorter than its diff:
```python
import functools

import jax
import jax.numpy as jnp
from jax import lax
from jax.experimental import pallas as pl
from jax.experimental.pallas import tpu as pltpu
from jax.sharding import PartitionSpec as P

MESH = pl.DeviceIdType.MESH
STEPS = 4
CLASSES = 8
ROWS = 64
PANELS = 8
PAD = 8
TILES = ROWS // 8
DT = 0.3
F0 = 0.3
K = DT / 12.0

PEERS = (
    (1, 0, 0), (0, 1, 0), (3, 0, 1), (2, 0, 0), (0, 1, 1),
    (1, 1, 0), (3, 1, 0), (2, 0, 1), (1, 0, 1), (3, 0, 0),
    (2, 1, 0), (1, 1, 1), (3, 1, 1), (2, 1, 1), (0, 0, 1),
)


def peer_of(me, step):
    x, z, c = me // 4, (me // 2) % 2, me % 2
    return ((x + step[0]) % 4) * 4 + ((z + step[1]) % 2) * 2 + (c + step[2]) % 2


def row_of(piece, d):
    tile = 2 + d // 4 if piece == 0 else d // 4 + 4 * (d // 8)
    return pl.multiple_of(tile * 8, 8)


def quarter_of(d):
    return d % 4


def kernel(
    copies, table, particles, classes, observed, gain, out,
    stage, cls, obs, gn, depth, state, flux, gathered0, gathered1, chosen, sent, got, g_halo,
    load_sem, halo_ss, halo_rs, g_ss, g_rs, ss1, rs1, ss2, rs2, self_sem,
):
    me, sp = lax.axis_index("dom"), lax.axis_index("space")
    gathered = (gathered0, gathered1)
    up, down = (sp + 7) % 8, (sp + 1) % 8

    loads = [
        pltpu.make_async_copy(classes, cls, load_sem.at[0]),
        pltpu.make_async_copy(particles, stage, load_sem.at[1]),
        pltpu.make_async_copy(gain, gn, load_sem.at[2]),
        pltpu.make_async_copy(observed, obs, load_sem.at[3]),
    ]
    for load in loads:
        load.start()

    barrier = pltpu.get_barrier_semaphore()
    for step in PEERS:
        pl.semaphore_signal(barrier, inc=1, device_id=(peer_of(me, step), sp), device_id_type=MESH)
    for other in (up, down):
        pl.semaphore_signal(barrier, inc=1, device_id=(me, other), device_id_type=MESH)

    lane = lax.broadcasted_iota(jnp.int32, (8, 128), 1)
    sublane = lax.broadcasted_iota(jnp.int32, (8, 128), 0)

    loads[0].wait()

    @pl.loop(0, TILES)
    def _(t):
        base = pl.multiple_of(t * 8, 8)
        for c in range(PANELS):
            kind = cls[pl.ds(base, 8), c * 128 : c * 128 + 128]
            d = jnp.zeros((8, 128), jnp.float32)
            for klass in range(CLASSES):
                d = jnp.where(kind == klass, table[klass], d)
            depth[c, pl.ds(base, 8), :] = d

    loads[1].wait()

    @pl.loop(0, 2 * TILES)
    def _(i):
        p, t = i // TILES, i % TILES
        base = pl.multiple_of(t * 8, 8)
        for c in range(PANELS):
            for f in range(3):
                v = stage[p, f, pl.ds(base, 8), c * 128 : c * 128 + 128]
                state[p, f, c, pl.ds(base + PAD, 8), :] = v
                if f == 2:
                    flux[p, c, pl.ds(base + PAD, 8), :] = depth[c, pl.ds(base, 8), :] * v

    loads[2].wait()
    loads[3].wait()

    def shifts(panels):
        ahead = [pltpu.roll(v, 127, 1) for v in panels]
        ahead2 = [pltpu.roll(v, 126, 1) for v in panels]
        behind = [pltpu.roll(v, 1, 1) for v in panels]
        behind2 = [pltpu.roll(v, 2, 1) for v in panels]
        found = []
        for c in range(PANELS):
            nxt, prv = (c + 1) % PANELS, (c - 1) % PANELS
            found.append((
                jnp.where(lane < 127, ahead[c], ahead[nxt]),
                jnp.where(lane >= 1, behind[c], behind[prv]),
                jnp.where(lane < 126, ahead2[c], ahead2[nxt]),
                jnp.where(lane >= 2, behind2[c], behind2[prv]),
            ))
        return found

    def height_of(p, base):
        panels = [
            depth[c, pl.ds(base, 8), :] * state[p, 1, c, pl.ds(base + PAD, 8), :]
            for c in range(PANELS)
        ]
        results = []
        for c, (a, b, a2, b2) in enumerate(shifts(panels)):
            ra = flux[p, c, pl.ds(base + PAD + 1, 8), :]
            rb = flux[p, c, pl.ds(base + PAD - 1, 8), :]
            ra2 = flux[p, c, pl.ds(base + PAD + 2, 8), :]
            rb2 = flux[p, c, pl.ds(base + PAD - 2, 8), :]
            div = 8.0 * ((a - b) + (ra - rb)) - ((a2 - b2) + (ra2 - rb2))
            h = state[p, 0, c, pl.ds(base + PAD, 8), :] - K * div
            g = gn[pl.ds(base, 8), c * 128 : c * 128 + 128]
            o = obs[pl.ds(base, 8), c * 128 : c * 128 + 128]
            results.append(h + g * (o - h))
        return results

    def height_tile(p, t, low, high):
        base = pl.multiple_of(t * 8, 8)
        inside = (base + sublane >= low) & (base + sublane < high)
        for c, h in enumerate(height_of(p, base)):
            old = state[p, 0, c, pl.ds(base + PAD, 8), :]
            state[p, 0, c, pl.ds(base + PAD, 8), :] = jnp.where(inside, h, old)

    def velocity_tile(p, t, low, high):
        base = pl.multiple_of(t * 8, 8)
        inside = (base + sublane >= low) & (base + sublane < high)
        panels = [state[p, 0, c, pl.ds(base + PAD, 8), :] for c in range(PANELS)]
        for c, (a, b, a2, b2) in enumerate(shifts(panels)):
            ra = state[p, 0, c, pl.ds(base + PAD + 1, 8), :]
            rb = state[p, 0, c, pl.ds(base + PAD - 1, 8), :]
            ra2 = state[p, 0, c, pl.ds(base + PAD + 2, 8), :]
            rb2 = state[p, 0, c, pl.ds(base + PAD - 2, 8), :]
            e = state[p, 1, c, pl.ds(base + PAD, 8), :]
            n = state[p, 2, c, pl.ds(base + PAD, 8), :]
            e_new = e - K * (8.0 * (a - b) - (a2 - b2)) + (DT * F0) * n
            n_new = n - K * (8.0 * (ra - rb) - (ra2 - rb2)) - (DT * F0) * e
            n_new = jnp.where(inside, n_new, n)
            state[p, 1, c, pl.ds(base + PAD, 8), :] = jnp.where(inside, e_new, e)
            state[p, 2, c, pl.ds(base + PAD, 8), :] = n_new
            flux[p, c, pl.ds(base + PAD, 8), :] = depth[c, pl.ds(base, 8), :] * n_new

    def halo_copies(k):
        return [
            pltpu.make_async_remote_copy(
                src_ref=sent.at[k, side],
                dst_ref=got.at[k, 1 - side],
                send_sem=halo_ss.at[k, side],
                recv_sem=halo_rs.at[k, 1 - side],
                device_id=(me, other),
                device_id_type=MESH,
            )
            for side, other in enumerate((up, down))
        ]

    def send_halo(k):
        @pl.loop(0, 2)
        def _(p):
            none = jnp.zeros((PANELS, 2, 128), jnp.float32)
            flux[p, :, PAD - 2 : PAD, :] = none
            flux[p, :, PAD + ROWS : PAD + ROWS + 2, :] = none
            for side, base, first in ((0, 0, 0), (1, ROWS - 8, 6)):
                for c, h in enumerate(height_of(p, base)):
                    f = flux[p, c, base + PAD : base + PAD + 8, :]
                    sent[k, side, c, pl.ds(p * 4, 2), :] = f[first : first + 2]
                    sent[k, side, c, pl.ds(p * 4 + 2, 2), :] = h[first : first + 2]

        for copy in halo_copies(k):
            copy.start()

    def take_halo(k):
        for copy in halo_copies(k):
            copy.wait_recv()
        top, bottom = sp > 0, sp < 7

        @pl.loop(0, 2)
        def _(p):
            for c in range(PANELS):
                first = flux[p, c, PAD : PAD + 1, :]
                second = flux[p, c, PAD + 1 : PAD + 2, :]
                last = flux[p, c, PAD + ROWS - 1 : PAD + ROWS, :]
                before = flux[p, c, PAD + ROWS - 2 : PAD + ROWS - 1, :]
                f_up = got[k, 0, c, pl.ds(p * 4, 2), :]
                f_down = got[k, 1, c, pl.ds(p * 4, 2), :]
                flux[p, c, PAD - 2 : PAD, :] = jnp.where(top, f_up, 0.0)
                flux[p, c, PAD + ROWS : PAD + ROWS + 2, :] = jnp.where(bottom, f_down, 0.0)
                cols = slice(c * 128, c * 128 + 128)
                for side, row, there, rest in (
                    (0, 0, PAD - 2, -first),
                    (0, 1, PAD - 1, 8.0 * first - second),
                    (1, 0, PAD + ROWS, before - 8.0 * last),
                    (1, 1, PAD + ROWS + 1, last),
                ):
                    near = row if side else row + 6
                    part = got[k, side, c, pl.ds(p * 4 + 2 + row, 1), :]
                    h = part - (1.0 - g_halo[side, near : near + 1, cols]) * (K * rest)
                    state[p, 0, c, there : there + 1, :] = jnp.where(bottom if side else top, h, 0.0)

    def inner(p):
        for k in range(1, STEPS + 1):

            @pl.loop((4 * k - 2) // 8, TILES - (4 * k - 2) // 8)
            def _(t):
                height_tile(p, t, 4 * k - 2, ROWS + 2 - 4 * k)

            @pl.loop(4 * k // 8, TILES - 4 * k // 8)
            def _(t):
                velocity_tile(p, t, 4 * k, ROWS - 4 * k)

    def outer(k):
        n = (4 * k - 2 + 7) // 8

        @pl.loop(0, 4 * n)
        def _(i):
            p, j = i // (2 * n), i % (2 * n)
            edge = j // n
            low = edge * (ROWS + 2 - 4 * k)
            height_tile(p, j + edge * (TILES - 2 * n), low, low + 4 * k - 2)

        m = (4 * k + 7) // 8

        @pl.loop(0, 4 * m)
        def _(i):
            p, j = i // (2 * m), i % (2 * m)
            edge = j // m
            low = edge * (ROWS - 4 * k)
            velocity_tile(p, j + edge * (TILES - 2 * m), low, low + 4 * k)

    def own_collect(piece):
        return pltpu.make_async_copy(
            state.at[:, :, pl.ds(2 * quarter_of(me), 2), pl.ds(PAD + row_of(piece, me), 8), :],
            gathered[piece].at[pl.ds(2 * me, 2)],
            self_sem.at[piece],
        )

    def collect(piece):
        for step in PEERS:
            d = peer_of(me, step)
            pltpu.make_async_remote_copy(
                src_ref=state.at[:, :, pl.ds(2 * quarter_of(d), 2), pl.ds(PAD + row_of(piece, d), 8), :],
                dst_ref=gathered[piece].at[pl.ds(2 * me, 2)],
                send_sem=ss1.at[piece],
                recv_sem=rs1.at[piece],
                device_id=(d, sp),
                device_id_type=MESH,
            ).start()
        own_collect(piece).start()

    def own_deliver(piece):
        return pltpu.make_async_copy(
            chosen.at[piece, pl.ds(2 * me, 2)],
            out.at[:, :, pl.ds(row_of(piece, me), 8), pl.ds(256 * quarter_of(me), 256)],
            self_sem.at[2 + piece],
        )

    def all_of(piece, sem):
        whole = gathered[piece].at[pl.ds(0, 30)]
        return pltpu.make_async_copy(whole, whole, sem.at[piece])

    def deliver(piece):
        all_of(piece, rs1).wait()
        own_collect(piece).wait()

        @pl.loop(0, 32)
        def _(j):
            source = copies[j]
            for f in range(3):
                for c in range(2):
                    chosen[piece, j, f, :, c * 128 : c * 128 + 128] = gathered[piece][source, f, c]

        for step in PEERS:
            d = peer_of(me, step)
            pltpu.make_async_remote_copy(
                src_ref=chosen.at[piece, pl.ds(2 * d, 2)],
                dst_ref=out.at[:, :, pl.ds(row_of(piece, me), 8), pl.ds(256 * quarter_of(me), 256)],
                send_sem=ss2.at[piece],
                recv_sem=rs2.at[piece],
                device_id=(d, sp),
                device_id_type=MESH,
            ).start()
        own_deliver(piece).start()

    g_copies = [
        pltpu.make_async_remote_copy(
            src_ref=gn.at[pl.ds(row, 8)],
            dst_ref=g_halo.at[1 - side, pl.ds(0, 8)],
            send_sem=g_ss.at[side],
            recv_sem=g_rs.at[1 - side],
            device_id=(me, other),
            device_id_type=MESH,
        )
        for side, other, row in ((0, up, 0), (1, down, ROWS - 8))
    ]

    pl.semaphore_wait(barrier, len(PEERS) + 2)
    send_halo(0)
    for copy in g_copies:
        copy.start()
    inner(0)
    inner(1)
    collect(0)
    for copy in g_copies:
        copy.wait_recv()
    for k in range(1, STEPS + 1):
        take_halo(k - 1)
        outer(k)
        if k < STEPS:
            send_halo(k)
    collect(1)
    deliver(0)
    deliver(1)
    for piece in range(2):
        all_of(piece, rs2).wait()
        own_deliver(piece).wait()
    for piece in range(2):
        all_of(piece, ss1).wait()
        all_of(piece, ss2).wait()
    for copy in g_copies:
        copy.wait_send()
    for k in range(STEPS):
        for copy in halo_copies(k):
            copy.wait_send()


def shards(particles, copies, depth_class, depth_table, observed, nudge_gain):
    f32 = jnp.float32
    sem = pltpu.SemaphoreType.DMA
    smem, anywhere = pl.BlockSpec(memory_space=pltpu.SMEM), pl.BlockSpec(memory_space=pl.ANY)
    return pl.pallas_call(
        kernel,
        out_shape=jax.ShapeDtypeStruct(particles.shape, f32),
        in_specs=[smem, smem, anywhere, anywhere, anywhere, anywhere],
        out_specs=anywhere,
        scratch_shapes=[
            pltpu.VMEM((2, 3, ROWS, 1024), f32),
            pltpu.VMEM((ROWS, 1024), jnp.int32),
            pltpu.VMEM((ROWS, 1024), f32),
            pltpu.VMEM((ROWS, 1024), f32),
            pltpu.VMEM((PANELS, ROWS, 128), f32),
            pltpu.VMEM((2, 3, PANELS, ROWS + 2 * PAD, 128), f32),
            pltpu.VMEM((2, PANELS, ROWS + 2 * PAD, 128), f32),
            pltpu.VMEM((32, 3, 2, 8, 128), f32),
            pltpu.VMEM((32, 3, 2, 8, 128), f32),
            pltpu.VMEM((2, 32, 3, 8, 256), f32),
            pltpu.VMEM((STEPS, 2, PANELS, 8, 128), f32),
            pltpu.VMEM((STEPS, 2, PANELS, 8, 128), f32),
            pltpu.VMEM((2, 8, 1024), f32),
            sem((4,)), sem((STEPS, 2)), sem((STEPS, 2)), sem((2,)), sem((2,)),
            sem((2,)), sem((2,)), sem((2,)), sem((2,)), sem((4,)),
        ],
        compiler_params=pltpu.CompilerParams(
            collective_id=0, has_side_effects=True, vmem_limit_bytes=40 * 2**20
        ),
    )(copies, depth_table, particles, depth_class, observed, nudge_gain)


def solution(mesh):
    placed = (
        P("dom", None, "space", None),
        P(),
        P("space", None),
        P(),
        P("space", None),
        P("space", None),
    )
    return jax.shard_map(
        shards, mesh=mesh, in_specs=placed, out_specs=P("dom", None, "space", None), check_vma=False
    )
```

time: 269 us -> 77.5 us (0.29)
  the two profiles are of different devices: /device:TPU:16 before, /device:TPU:1 now
where the time goes in v1:
time: 77.5 us; the launch traced here: 77.3 us
  Pallas kernels  70.5 us (91%)
  local copies, waits for them, and re-layouts  6.71 us (9%)
    pallas_call x1, Pallas kernels, shards(): pl.pallas_call(kernel, out_shape=jax.ShapeDtypeStruct(particles.shape, f3...  70.5 us
    unnamed x13, local copies, waits for them, and re-layouts  6.71 us

profile of v1, /device:TPU:1, one launch (start us, length us, event | category | flops | bytes accessed | tf_op | source)
XLA Modules:
  0.0 77.3 jit_solution(9741776158767795314)
XLA Ops:
  0.0 0.0 copy-start
  0.0 1.4 %copy-done = f32[2,3,64,1024]{3,2,1,0:T(8,128)S(1)} copy-done((f32[2,3,64,1024]{3,2,1,0:T(8,128)S(1)}, f32[2,3,64,1024]{3,2,1,0:T(8,128)}, u32[]{:S(2)}) %copy-start) | copy-done | bytes 1572888
  1.4 0.0 copy-start.1
  1.4 0.9 %copy-done.1 = s32[64,1024]{1,0:T(8,128)S(1)} copy-done((s32[64,1024]{1,0:T(8,128)S(1)}, s32[64,1024]{1,0:T(8,128)}, u32[]{:S(2)}) %copy-start.1) | copy-done | bytes 262168
  2.4 0.0 copy-start.2
  2.4 0.9 %copy-done.2 = f32[64,1024]{1,0:T(8,128)S(1)} copy-done((f32[64,1024]{1,0:T(8,128)S(1)}, f32[64,1024]{1,0:T(8,128)}, u32[]{:S(2)}) %copy-start.2) | copy-done | bytes 262168
  3.3 0.0 copy-start.3
  3.3 0.9 %copy-done.3 = f32[64,1024]{1,0:T(8,128)S(1)} copy-done((f32[64,1024]{1,0:T(8,128)S(1)}, f32[64,1024]{1,0:T(8,128)}, u32[]{:S(2)}) %copy-start.3) | copy-done | bytes 262168
  4.3 0.0 copy-start.4
  4.3 0.7 copy-done.4
  4.9 0.0 copy-start.5
  4.9 0.7 copy-done.5
  5.6 70.5 %shard_map.64 = f32[2,3,64,1024]{3,2,1,0:T(8,128)S(1)} custom-call(s32[32]{0:T(128)S(1)} %copy-done.4, f32[8]{0:T(128)S(1)} %copy-done.5, f32[2,3,64,1024]{3,2,1,0:T(8,128)S(1)} %copy-done, s32[64,1024]{1,0:T(8,128)S(1)} %copy-done.1, f32[64,1024]{1,0:T(8,128)S(1)} %copy-done.2, f32[64,1024]{1,0:T(8,128)S(1)} %copy-done.3), custom_call_target="tpu_custom_call" | custom-call | tf_op jit(solution)/shard_map/pallas_call | solution.py:342
  76.1 1.1 %copy.8 = f32[2,3,64,1024]{3,2,1,0:T(8,128)} copy(f32[2,3,64,1024]{3,2,1,0:T(8,128)S(1)} %shard_map.64) | data formatting | bytes 3145728
Async XLA Ops:
  0.0 1.4 %copy-start = (f32[2,3,64,1024]{3,2,1,0:T(8,128)S(1)}, f32[2,3,64,1024]{3,2,1,0:T(8,128)}, u32[]{:S(2)}) copy-start(f32[2,3,64,1024]{3,2,1,0:T(8,128)} %particles.1) | copy-start | bytes 4718596
  1.4 0.9 %copy-start.1 = (s32[64,1024]{1,0:T(8,128)S(1)}, s32[64,1024]{1,0:T(8,128)}, u32[]{:S(2)}) copy-start(s32[64,1024]{1,0:T(8,128)} %classes.1) | copy-start | bytes 786436
  2.4 0.9 %copy-start.2 = (f32[64,1024]{1,0:T(8,128)S(1)}, f32[64,1024]{1,0:T(8,128)}, u32[]{:S(2)}) copy-start(f32[64,1024]{1,0:T(8,128)} %observed.1) | copy-start | bytes 786436
  3.3 0.9 %copy-start.3 = (f32[64,1024]{1,0:T(8,128)S(1)}, f32[64,1024]{1,0:T(8,128)}, u32[]{:S(2)}) copy-start(f32[64,1024]{1,0:T(8,128)} %gain.1) | copy-start | bytes 786436
  4.3 0.7 copy-start.4
  4.9 0.7 copy-start.5
